TPU v7x, 256 devices: a whole 4x4x8 slice. The times are simulated.
256 devices in a mesh: pair: 16 (over z, core), ri: 16 (over y, x).
Axes of the slice: x: 4, y: 4, z: 8, core: 2. Of those that a mesh axis runs over, the one named last changes fastest.
Arguments:
- three_center: bfloat16 [16, 2048, 16, 384], P('pair', 'ri'), may hold values from -6 to 6
- green: bfloat16 [16, 16, 64, 64], P('pair'), may hold values from -0.3125 to 0.3125
- screened: bfloat16 [2048, 2048], P('ri'), may hold values from -0.00015258789 to 0.00015258789
- block_tile: int32 [16, 6], replicated, may hold values from 0 to 15, all different within a row
- sigma_owner: int32 [16], replicated, may hold values from 0 to 15, as said below
Outputs:
- sigma: float32 [16, 16, 16], P('pair')
Inputs may be any that keep to these rules, and one draw needn't show every extreme that they name: `block_tile`: each row names 6 different tiles; every one of the 16 tiles is named by some region. `sigma_owner`: each owner slot appears once.
All inputs are finite; a program needn't handle non-finite values.
Results may differ from a plain program's by a relative error of at most 0.0041.
Values may be sent and summed in bfloat16 or wider, within the bound.
A program may use at most 128 MiB of HBM per device.

v0:
```python
import jax
import jax.numpy as jnp
from jax import lax
from jax.sharding import PartitionSpec as P


def on_device(three_center, green, screened, block_tile, sigma_owner):
    region = lax.axis_index("pair")
    region_count = lax.axis_size("pair")
    tiles_count = block_tile.shape[1]
    tile_size = green.shape[-1]
    own_tiles = lax.dynamic_index_in_dim(block_tile, region, 0, keepdims=False)
    whole = lax.all_gather(green, "pair", axis=0, tiled=True)
    selected = jnp.take(jnp.take(whole, own_tiles, axis=0), own_tiles, axis=1)
    columns = tiles_count * tile_size
    coupling = selected.transpose(0, 2, 1, 3).reshape(columns, columns)
    local = three_center[0]
    rows_local, width_rows, _ = local.shape
    half = jnp.dot(
        local.reshape(rows_local * width_rows, columns),
        coupling,
        preferred_element_type=jnp.float32,
    )
    half = half.astype(jnp.bfloat16).reshape(local.shape)
    block_rows = lax.all_gather(local, "ri", axis=0, tiled=True)
    flat_block = block_rows.reshape(block_rows.shape[0], -1)
    summed = jnp.dot(screened, flat_block, preferred_element_type=jnp.float32)
    weighted = summed.astype(jnp.bfloat16).reshape(local.shape)
    partial_tile = -jnp.einsum("pmc,pnc->mn", half, weighted, preferred_element_type=jnp.float32)
    sigma_tile = lax.psum(partial_tile, "ri")
    destination = lax.dynamic_index_in_dim(sigma_owner, region, 0, keepdims=False)
    is_target = jnp.arange(region_count, dtype=jnp.int32) == destination
    routed = jnp.where(is_target[:, None, None], sigma_tile[None, :, :], jnp.float32(0.0))
    arrived = lax.all_to_all(routed, "pair", split_axis=0, concat_axis=0, tiled=True)
    return jnp.sum(arrived, axis=0, keepdims=True)


def solution(mesh):
    in_specs = (P("pair", "ri", None, None), P("pair", None, None, None), P("ri", None), P(), P())
    out_specs = P("pair", None, None)
    return jax.shard_map(
        on_device, mesh=mesh, in_specs=in_specs, out_specs=out_specs, check_vma=False
    )
```

profile of v0, /device:TPU:1, one launch (start us, length us, event | category | flops | bytes accessed | tf_op | source)
XLA Modules:
  0.0 316.3 jit_solution(11808794537802585204)
XLA Ops:
  6.5 0.0 copy-start
  6.5 0.0 all-gather.4.cloned.1.call-start
  6.5 0.7 all-gather.4.cloned.1.call-update
  7.3 0.0 all-gather.6.cloned.1.call-start
  7.3 0.7 all-gather.6.cloned.1.call-update
  8.0 0.2 dynamic-slice_reduce_fusion
  8.2 0.6 dynamic_slice.8
  8.8 0.6 iota_compare_fusion
  9.5 46.0 %all-gather.4.cloned.1.call-done = bf16[16,16,64,64]{3,2,1,0:T(8,128)(2,1)} async-done(((bf16[1,16,64,64]{3,2,1,0:T(8,128)(2,1)}), bf16[16,16,64,64]{3,2,1,0:T(8,128)(2,1)}) %all-gather.4.cloned.1.call-update) | async-done | bytes 2097168 | tf_op jit(solution)/shard_map/all_gather | solution.py:13
  55.6 3.0 gather_fusion
  58.6 1.4 broadcast_select_fusion
  60.0 2.1 gather_fusion.1
  62.1 0.0 copy-start.1
  62.1 0.1 select_bitcast_fusion
  62.3 0.4 copy.15
  62.7 0.5 reshape.51
  63.2 0.4 copy-done.1
  63.5 2.3 fusion
  65.8 1.9 copy.16
  67.7 147.7 %all-gather.6.cloned.1.call-done = bf16[1,2048,16,384]{3,2,0,1:T(8,128)(2,1)} async-done(((bf16[1,128,16,384]{3,2,0,1:T(8,128)(2,1)}), bf16[1,2048,16,384]{3,2,0,1:T(8,128)(2,1)}) %all-gather.6.cloned.1.call-update) | async-done | bytes 25165840 | tf_op jit(solution)/shard_map/all_gather | solution.py:25
  215.4 25.5 %copy.18 = bf16[256,8,16,384]{3,1,2,0:T(8,128)(2,1)} copy(bf16[256,8,16,384]{3,2,1,0:T(8,128)(2,1)} %bitcast.30) | data formatting | bytes 50331648
  240.9 11.6 %convolution_convert_fusion = bf16[128,6144]{1,0:T(8,128)(2,1)S(1)} fusion(bf16[128,2048]{1,0:T(8,128)(2,1)S(1)} %copy-done, bf16[2048,6144]{1,0:T(8,128)(2,1)} %bitcast.29), kind=kOutput, calls=%fused_computation.2 | convolution fusion | flops 3222011904 | bytes 27262976 | tf_op jit(solution)/shard_map/dot_general | solution.py:27
  252.5 0.3 copy.19
  252.8 0.7 fusion.1
  253.5 32.0 %psum.7 = f32[16,16]{1,0:T(8,128)S(1)} all-reduce(f32[16,16]{1,0:T(8,128)S(1)} %fusion.1), channel_id=1, replica_groups=mesh['pair'=16,'ri'=16] {'ri'}, use_global_device_ids=true, to_apply=%region_0.1 | all-reduce | flops 256 | bytes 2048 | tf_op jit(solution)/shard_map/psum | solution.py:30
  285.6 0.1 broadcast_select_fusion.1
  285.7 0.1 reshape.76
  285.8 21.8 %all_to_all.5 = f32[16,1,256]{2,1,0:T(1,128)S(1)} all-to-all(f32[16,1,256]{2,1,0:T(1,128)S(1)} %reshape.76), channel_id=1, replica_groups=mesh['pair'=16,'ri'=16] {'pair'}, dimensions={0} | all-to-all | bytes 32768 | tf_op jit(solution)/shard_map/all_to_all | solution.py:34
  307.6 0.5 broadcast.63
  308.1 0.7 reduce.3
  308.8 0.1 reshape.77
  308.9 0.6 reduce_sum.9
  (8 shorter events, 0.0 us)
Async XLA Ops:
  6.5 234.4 %copy-start = (bf16[128,2048]{1,0:T(8,128)(2,1)S(1)}, bf16[128,2048]{1,0:T(8,128)(2,1)}, u32[]{:S(2)}) copy-start(bf16[128,2048]{1,0:T(8,128)(2,1)} %param.7) | copy-start | bytes 1572868
  6.5 1.5 copy-start.2
  6.5 1.7 copy-start.3
  6.5 49.0 %all-gather.4.cloned.1.call-start = ((), (), s32[]{:S(2)}) async-start(), calls=%async_computation.1 | async-start | bytes 4456448 | tf_op jit(solution)/shard_map/all_gather | solution.py:13
  7.3 208.1 %all-gather.6.cloned.1.call-start = ((), (), s32[]{:S(2)}) async-start(), calls=%async_computation.2 | async-start | bytes 26738688 | tf_op jit(solution)/shard_map/all_gather | solution.py:25
  62.1 1.4 copy-start.1
Sparse Core Ops, SparseCore 0:
  9.2 46.3 all-gather.3
  58.0 157.3 all-gather.5
where the time goes:
time: 317 us; the launch traced here: 316 us
  waiting for transfers between devices  195 us (62%)
  blocking collectives  53.8 us (17%)
  local copies, waits for them, and re-layouts  35.6 us (11%)
  matrix products  14.6 us (5%)
  between operations  13.6 us (4%)
  other arithmetic  3.63 us (1%)
    all_gather x1, waiting for transfers between devices, on_device(): block_rows = lax.all_gather(local, 'ri', axis=0, tiled=True)  148 us
    all_gather x1, waiting for transfers between devices, on_device(): whole = lax.all_gather(green, 'pair', axis=0, tiled=True)  46 us
    psum x1, blocking collectives, on_device(): sigma_tile = lax.psum(partial_tile, 'ri')  32 us
    unnamed x12, local copies, waits for them, and re-layouts  26.4 us
    all_to_all x1, blocking collectives, on_device(): lax.all_to_all(routed, 'pair', split_axis=0, concat_axis=0, tiled=True)  21.8 us
    dot_general x1, matrix products, on_device(): summed = jnp.dot(screened, flat_block, preferred_element_type=jnp.float32)  11.6 us
  transfers between devices with their start and end apart: 2, of which 2 were waited for; matrix products, arithmetic and copies ran while one was open for 4% of the time, Pallas kernels for 0%

commit v1 on v0

v1 whole, which is shorter than its diff:
```python
import functools

import jax
import jax.numpy as jnp
from jax import lax
from jax.experimental import pallas as pl
from jax.experimental.pallas import tpu as pltpu
from jax.sharding import PartitionSpec as P

MESH = pl.DeviceIdType.MESH
F32, BF16 = jnp.float32, jnp.bfloat16


def remote(src, dst, send_sem, recv_sem, device):
    return pltpu.make_async_remote_copy(
        src_ref=src, dst_ref=dst, send_sem=send_sem, recv_sem=recv_sem, device_id=device, device_id_type=MESH
    )


def wait_bytes(ref, sem):
    pltpu.make_async_copy(ref, ref, sem).wait()


def iota2(shape, dim):
    return lax.broadcasted_iota(jnp.int32, shape, dim)


NT = (((1,), (1,)), ((), ()))
ORDER = (0, 1, 3, 2)


def kernel(
    tiles_hbm, owner_hbm, three_hbm, green_hbm, screened_hbm, out_ref,
    tiles_ref, owner_ref, three, green, by_mu, place, stage, t_out, h_out, columns, rows, weighted, halves,
    g_wide, g_out, g_in, g_own, g_all, partials, totals,
    local_sem, a_send, a_recv, t_send, t_recv, h_send, h_recv,
    ring_send, ring_recv, sib_send, sib_recv, own_send, own_recv,
    g_send, g_recv, c_send, c_recv, f_send, f_recv,
):
    pair, ri = lax.axis_index("pair"), lax.axis_index("ri")
    z, core = pair // 2, pair % 2
    y, x = ri // 4, ri % 4
    sibling = (z * 2 + 1 - core, ri)

    def chip(step):
        return (z + step + 8) % 8

    def neighbour(step):
        return (chip(step) * 2 + core, ri)

    def plane_peer(step):
        return (ri + step) % 16

    def pair_peer(step):
        return (pair + step) % 16

    load_three = pltpu.make_async_copy(three_hbm.at[0], three, local_sem.at[0])
    load_green = pltpu.make_async_copy(green_hbm.at[0], green, local_sem.at[1])
    load_tiles = pltpu.make_async_copy(tiles_hbm, tiles_ref, local_sem.at[3])
    load_owner = pltpu.make_async_copy(owner_hbm, owner_ref, local_sem.at[4])
    mine = pl.ds(pl.multiple_of(ri * 16, 16), 16)
    row_piece = screened_hbm.at[
        pl.ds(pl.multiple_of(z * 16, 16), 16), pl.ds(pl.multiple_of(core * 1024, 1024), 1024)
    ]
    load_rows = pltpu.make_async_copy(row_piece, rows.at[z, core, mine], local_sem.at[2])
    load_three.start()
    load_tiles.start()
    load_green.start()
    load_rows.start()
    load_owner.start()
    barrier = pltpu.get_barrier_semaphore()

    @pl.loop(1, 16)
    def _(step):
        pl.semaphore_signal(barrier, inc=1, device_id=(pair, plane_peer(step)), device_id_type=MESH)
        pl.semaphore_signal(barrier, inc=1, device_id=(pair_peer(step), ri), device_id_type=MESH)

    first, second = iota2((256, 256), 0), iota2((256, 256), 1)
    swap = ((first % 16) * 16 + first // 16 == second).astype(BF16)
    spot, lane = iota2((768, 384), 0), iota2((768, 384), 1)
    wanted = (spot // 48) * 24 + spot % 24 == lane
    for odd in range(2):
        place[odd] = (wanted & ((spot % 48) // 24 == odd)).astype(BF16)
    load_three.wait()

    @pl.loop(0, 8)
    def _(chunk):
        at = pl.ds(pl.multiple_of(chunk * 16, 16), 16)
        block = three[at].reshape(256, 384)
        by_mu[:, at] = jnp.dot(swap, block, preferred_element_type=F32).astype(BF16).reshape(16, 16, 384)

    def arrange(out):
        @pl.loop(0, 8)
        def _(two):
            block = lax.dot_general(place[0], by_mu[2 * two], NT, preferred_element_type=F32)
            block += lax.dot_general(place[1], by_mu[2 * two + 1], NT, preferred_element_type=F32)
            out[:, pl.ds(pl.multiple_of(two * 48, 16), 48)] = block.astype(BF16).reshape(16, 48, 128)

    arrange(stage)

    load_green.wait()
    load_tiles.wait()
    load_owner.wait()
    green_rows = pl.ds(pl.multiple_of(y * 16, 16), 16)

    @pl.loop(0, 16)
    def _(region):
        for j in range(6):
            g_wide[j, region] = green[tiles_ref[j, region], green_rows, :]

    source, target = iota2((64, 128), 0), iota2((64, 128), 1)
    picked = jnp.zeros((256, 128), F32)
    for j in range(6):
        spots = ((target // 16 == j) & (source == x * 16 + target % 16)).astype(BF16)
        picked += jnp.dot(g_wide[j].reshape(256, 64), spots, preferred_element_type=F32)
    g_out[...] = picked.astype(BF16).reshape(16, 16, 128)
    g_in[pair] = g_out[pair]
    load_rows.wait()
    pl.semaphore_wait(barrier, 30)

    for q in ORDER:
        for dx in range(4):
            if q or dx:
                peer = ((y + 4 - q) % 4) * 4 + (x + dx) % 4
                remote(row_piece, rows.at[z, core, mine], a_send, a_recv.at[q], (pair, peer)).start()

    @pl.loop(1, 16)
    def _(step):
        peer = pair_peer(step)
        remote(g_out.at[peer], g_in.at[pair], g_send, g_recv, (peer, ri)).start()

    own_columns = pl.ds(pl.multiple_of(ri * 128, 128), 128)
    eye = (iota2((128, 128), 0) == iota2((128, 128), 1)).astype(BF16)

    @pl.loop(0, 16)
    def _(peer):
        t_out[peer] = lax.dot_general(eye, stage[peer], NT, preferred_element_type=F32).astype(BF16)

    def part_of(step, which, q, count=64):
        return rows.at[chip(step), which, pl.ds(pl.multiple_of(((y + q) % 4) * 64, 64), count)]

    def ring(way, step, q):
        i = (1 - way) // 2
        ref = part_of(-way * (step - 1), core, q)
        return remote(ref, ref, ring_send.at[i, step - 1, q], ring_recv.at[i, step - 1, q], neighbour(way))

    def side(way, step, q):
        i = (1 - way) // 2
        ref = part_of(-way * step, core, q)
        return remote(ref, ref, sib_send.at[i, step - 1, q], sib_recv.at[i, step - 1, q], sibling)

    def own_side(q):
        ref = part_of(0, core, q)
        return remote(ref, ref, own_send.at[q], own_recv.at[q], sibling)

    def parts_at(way, step):
        if step < 4:
            return ORDER
        return ORDER[0:2] if way == 1 else ORDER[2:4]

    def begin(q):
        wait_bytes(part_of(0, core, q, 64 if q else 48), a_recv.at[q])
        for way in (1, -1):
            ring(way, 1, q).start()
        own_side(q).start()

    begin(ORDER[0])

    wait_bytes(g_in.at[pl.ds(0, 15)], g_recv)
    for k in range(6):
        g_own[k] = g_in[tiles_ref[k, pair]]
    g_place = g_all.at[:, y, :, pl.ds(pl.multiple_of(x * 128, 128), 128)]

    def share(step):
        return remote(g_own, g_place, c_send.at[step], c_recv.at[step], (pair, plane_peer(step)))

    @pl.loop(1, 16)
    def _(step):
        share(step).start()

    g_all[:, y, :, pl.ds(pl.multiple_of(x * 128, 128), 128)] = g_own[...]

    @pl.loop(1, 16)
    def _(step):
        peer = plane_peer(step)
        remote(t_out.at[peer], columns.at[own_columns], t_send, t_recv, (pair, peer)).start()

    columns[own_columns, :] = t_out[ri]
    for q in ORDER[1:]:
        begin(q)

    def serve(step):
        for q in ORDER:
            for way in (1, -1):
                if q in parts_at(way, step):
                    wait_bytes(part_of(-way * step, core, q), ring_recv.at[(1 - way) // 2, step - 1, q])
                    if step < 4 and q in parts_at(way, step + 1):
                        ring(way, step + 1, q).start()
                    side(way, step, q).start()

    def sides_in(way, step):
        for q in parts_at(way, step):
            wait_bytes(part_of(-way * step, 1 - core, q), sib_recv.at[(1 - way) // 2, step - 1, q])

    def process(step):
        piece = chip(step)
        total = jnp.dot(rows[piece, 0], columns[0:1024], preferred_element_type=F32)
        total += jnp.dot(rows[piece, 1], columns[1024:2048], preferred_element_type=F32)
        at = pl.ds(pl.multiple_of(piece * 16, 16), 16)
        weighted[:, at] = total.astype(BF16).reshape(16, 16, 384)

    serve(1)

    @pl.loop(1, 16)
    def _(step):
        share(step).wait_recv()

    source, target = iota2((512, 384), 0), iota2((512, 384), 1)
    order = (
        (source // 128 == (target // 16) % 4) & ((source % 128) // 16 == target // 64) & (source % 16 == target % 16)
    ).astype(BF16)
    coupling = jnp.dot(g_all[...].reshape(384, 512), order, preferred_element_type=F32).astype(BF16)
    for odd in range(2):
        place[odd] = lax.dot_general(place[odd], coupling, NT, preferred_element_type=F32).astype(BF16)
    arrange(h_out)
    own_lanes = pl.ds(pl.multiple_of(ri * 128, 128), 128)

    @pl.loop(1, 16)
    def _(step):
        peer = plane_peer(step)
        remote(h_out.at[peer], halves.at[:, own_lanes], h_send, h_recv, (pair, peer)).start()

    halves[:, own_lanes] = h_out[ri]

    serve(2)
    wait_bytes(columns.at[pl.ds(0, 1920)], t_recv)
    for q in ORDER:
        wait_bytes(part_of(0, 1 - core, q), own_recv.at[q])
    process(0)
    for step in (1, 2):
        for way in (1, -1):
            sides_in(way, step)
            process(-way * step)
    serve(3)
    for way in (1, -1):
        sides_in(way, 3)
        process(-3 * way)
    serve(4)
    for way in (1, -1):
        sides_in(way, 4)
    process(4)
    wait_bytes(halves.at[:, pl.ds(0, 1920)], h_recv)
    gram = jnp.dot(halves[...], weighted[...].reshape(2048, 384), preferred_element_type=F32)

    masked = jnp.where(iota2((384, 384), 0) % 24 == iota2((384, 384), 1) % 24, gram, 0.0)
    fold = (iota2((16, 384), 1) // 24 == iota2((16, 384), 0)).astype(F32)
    folded = jnp.dot(fold, masked, preferred_element_type=F32, precision=lax.Precision.HIGHEST)
    spread = (iota2((384, 128), 0) // 24 == iota2((384, 128), 1) % 16).astype(F32)
    wide = jnp.dot(folded, spread, preferred_element_type=F32, precision=lax.Precision.HIGHEST)
    keep = iota2((16, 128), 1) // 16 == iota2((16, 128), 0) % 8
    partials[ri] = jnp.sum(jnp.where(keep, wide, 0.0).reshape(2, 8, 128), axis=1)

    @pl.loop(1, 16)
    def _(step):
        remote(partials.at[ri], partials.at[ri], f_send.at[0], f_recv.at[0], (pair, plane_peer(step))).start()

    wait_bytes(partials.at[pl.ds(0, 15)], f_recv.at[0])
    totals[pair] = -jnp.sum(partials[...], axis=0)

    @pl.loop(1, 16)
    def _(step):
        remote(totals.at[pair], totals.at[pair], f_send.at[1], f_recv.at[1], (pair_peer(step), ri)).start()

    wait_bytes(rows.at[z, core, pl.ds(0, 240)], a_send)
    wait_bytes(columns.at[pl.ds(0, 1920)], t_send)
    wait_bytes(halves.at[:, pl.ds(0, 1920)], h_send)
    wait_bytes(g_in.at[pl.ds(0, 15)], g_send)
    for q in ORDER:
        own_side(q).wait_send()
    for step in (1, 2, 3, 4):
        for way in (1, -1):
            for q in parts_at(way, step):
                ring(way, step, q).wait_send()
                side(way, step, q).wait_send()

    @pl.loop(1, 16)
    def _(step):
        share(step).wait_send()

    wait_bytes(partials.at[pl.ds(0, 15)], f_send.at[0])
    wait_bytes(totals.at[pl.ds(0, 15)], f_send.at[1])
    wait_bytes(totals.at[pl.ds(0, 15)], f_recv.at[1])
    result = jnp.zeros((2, 128), F32)
    for region in range(16):
        result += jnp.where(owner_ref[region] == pair, totals[region], 0.0)
    again = jnp.broadcast_to(result[:, None, :], (2, 8, 128)).reshape(16, 128)
    narrow = (iota2((128, 16), 0) % 16 == iota2((128, 16), 1)).astype(F32)
    out_ref[0] = jnp.dot(
        jnp.where(keep, again, 0.0), narrow, preferred_element_type=F32, precision=lax.Precision.HIGHEST
    )


def on_device(three_center, green, screened, block_tile, sigma_owner):
    dma = pltpu.SemaphoreType.DMA
    return pl.pallas_call(
        kernel,
        out_shape=jax.ShapeDtypeStruct((1, 16, 16), F32),
        in_specs=[pl.BlockSpec(memory_space=pltpu.HBM)] * 5,
        out_specs=pl.BlockSpec(memory_space=pltpu.VMEM),
        scratch_shapes=[
            pltpu.SMEM((6, 16), jnp.int32),
            pltpu.SMEM((16,), jnp.int32),
            pltpu.VMEM((128, 16, 384), BF16),
            pltpu.VMEM((16, 64, 64), BF16),
            pltpu.VMEM((16, 128, 384), BF16),
            pltpu.VMEM((2, 768, 384), BF16),
            pltpu.VMEM((16, 384, 128), BF16),
            pltpu.VMEM((16, 128, 384), BF16),
            pltpu.VMEM((16, 384, 128), BF16),
            pltpu.VMEM((2048, 384), BF16),
            pltpu.VMEM((8, 2, 256, 1024), BF16),
            pltpu.VMEM((16, 128, 384), BF16),
            pltpu.VMEM((384, 2048), BF16),
            pltpu.VMEM((6, 16, 16, 64), BF16),
            pltpu.VMEM((16, 16, 128), BF16),
            pltpu.VMEM((16, 16, 128), BF16),
            pltpu.VMEM((6, 16, 128), BF16),
            pltpu.VMEM((6, 4, 16, 512), BF16),
            pltpu.VMEM((16, 2, 128), F32),
            pltpu.VMEM((16, 2, 128), F32),
            dma((5,)), dma, dma((4,)), dma, dma, dma, dma,
            dma((2, 4, 4)), dma((2, 4, 4)), dma((2, 4, 4)), dma((2, 4, 4)), dma((4,)), dma((4,)),
            dma, dma, dma((16,)), dma((16,)), dma((2,)), dma((2,)),
        ],
        compiler_params=pltpu.CompilerParams(
            collective_id=0, has_side_effects=True, vmem_limit_bytes=60 * 1024 * 1024
        ),
    )(block_tile.T, sigma_owner, three_center, green, screened)


def solution(mesh):
    in_specs = (P("pair", "ri", None, None), P("pair", None, None, None), P("ri", None), P(), P())
    return jax.shard_map(
        on_device, mesh=mesh, in_specs=in_specs, out_specs=P("pair", None, None), check_vma=False
    )
```

time: 317 us -> 82.2 us (0.26)
  waiting for transfers between devices: 195 us -> 0 us
  Pallas kernels: 0 us -> 80.7 us
  blocking collectives: 53.8 us -> 0 us
  local copies, waits for them, and re-layouts: 35.6 us -> 1.3 us
  matrix products: 14.6 us -> 0 us
  between operations: 13.6 us -> 0.01 us
  other arithmetic: 3.63 us -> 0 us
    all_gather x2 -> x0, waiting for transfers between devices: 194 us -> none  [the longest x1 148 us: on_device(): block_rows = lax.all_gather(local, 'ri', axis=0, tiled=True)]
    pallas_call x0 -> x1, Pallas kernels: none -> 80.7 us  [on_device(): pl.pallas_call(kernel, out_shape=jax.ShapeDtypeStruct((1, 16, 16), F32),...]
    psum x1 -> x0, blocking collectives: 32 us -> none  [on_device(): sigma_tile = lax.psum(partial_tile, 'ri')]
    unnamed x12 -> x1, local copies, waits for them, and re-layouts: 26.4 us -> 1.3 us
    all_to_all x1 -> x0, blocking collectives: 21.8 us -> none  [on_device(): lax.all_to_all(routed, 'pair', split_axis=0, concat_axis=0, tiled=True)]
    dot_general x3 -> x0, matrix products: 14.6 us -> none  [the longest x1 11.6 us: on_device(): summed = jnp.dot(screened, flat_block, preferred_element_type=jnp.float32)]
    gather x2 -> x0, local copies, waits for them, and re-layouts: 5.1 us -> none  [on_device(): selected = jnp.take(jnp.take(whole, own_tiles, axis=0), own_tiles, axis=1)]
  transfers between devices with their start and end apart: 2 -> 0, of which waited for: 2 -> 0; matrix products, arithmetic and copies ran while one was open for 4% -> 0% of each run, Pallas kernels for 0% -> 0%
where the time goes in v1:
time: 82.2 us; the launch traced here: 82 us
  Pallas kernels  80.7 us (98%)
  local copies, waits for them, and re-layouts  1.3 us (2%)
    pallas_call x1, Pallas kernels, on_device(): pl.pallas_call(kernel, out_shape=jax.ShapeDtypeStruct((1, 16, 16), F32),...  80.7 us

profile of v1, /device:TPU:1, one launch (start us, length us, event | category | flops | bytes accessed | tf_op | source)
XLA Modules:
  0.0 82.0 jit_solution(12331304572094237491)
XLA Ops:
  0.0 80.7 %shard_map.55 = f32[1,16,16]{2,1,0:T(8,128)} custom-call(s32[6,16]{1,0:T(8,128)} %bitcast.1, s32[16]{0:T(128)} %owner_hbm.1, bf16[1,128,16,384]{3,2,1,0:T(8,128)(2,1)} %three_hbm.1, bf16[1,16,64,64]{3,2,1,0:T(8,128)(2,1)} %green_hbm.1, bf16[128,2048]{1,0:T(8,128)(2,1)} %screened_hbm.1), custom_call_target="tpu_custom_call" | custom-call | tf_op jit(solution)/shard_map/pallas_call | solution.py:305
  80.7 1.3 %copy.7 = f32[1,16,16]{2,1,0:T(8,128)} copy(f32[1,16,16]{2,1,0:T(8,128)} %shard_map.55) | data formatting | bytes 2048

commit v2 on v1

--- a/solution.py
+++ b/solution.py
@@ -31,7 +31,7 @@
 
 def kernel(
     tiles_hbm, owner_hbm, three_hbm, green_hbm, screened_hbm, out_ref,
-    tiles_ref, owner_ref, three, green, by_mu, place, stage, t_out, h_out, columns, rows, weighted, halves,
+    tiles_ref, owner_ref, three, green, by_mu, left, stage, t_out, h_out, columns, rows, weighted, halves,
     g_wide, g_out, g_in, g_own, g_all, partials, totals,
     local_sem, a_send, a_recv, t_send, t_recv, h_send, h_recv,
     ring_send, ring_recv, sib_send, sib_recv, own_send, own_recv,
@@ -75,29 +75,6 @@
         pl.semaphore_signal(barrier, inc=1, device_id=(pair, plane_peer(step)), device_id_type=MESH)
         pl.semaphore_signal(barrier, inc=1, device_id=(pair_peer(step), ri), device_id_type=MESH)
 
-    first, second = iota2((256, 256), 0), iota2((256, 256), 1)
-    swap = ((first % 16) * 16 + first // 16 == second).astype(BF16)
-    spot, lane = iota2((768, 384), 0), iota2((768, 384), 1)
-    wanted = (spot // 48) * 24 + spot % 24 == lane
-    for odd in range(2):
-        place[odd] = (wanted & ((spot % 48) // 24 == odd)).astype(BF16)
-    load_three.wait()
-
-    @pl.loop(0, 8)
-    def _(chunk):
-        at = pl.ds(pl.multiple_of(chunk * 16, 16), 16)
-        block = three[at].reshape(256, 384)
-        by_mu[:, at] = jnp.dot(swap, block, preferred_element_type=F32).astype(BF16).reshape(16, 16, 384)
-
-    def arrange(out):
-        @pl.loop(0, 8)
-        def _(two):
-            block = lax.dot_general(place[0], by_mu[2 * two], NT, preferred_element_type=F32)
-            block += lax.dot_general(place[1], by_mu[2 * two + 1], NT, preferred_element_type=F32)
-            out[:, pl.ds(pl.multiple_of(two * 48, 16), 48)] = block.astype(BF16).reshape(16, 48, 128)
-
-    arrange(stage)
-
     load_green.wait()
     load_tiles.wait()
     load_owner.wait()
@@ -108,32 +85,56 @@
         for j in range(6):
             g_wide[j, region] = green[tiles_ref[j, region], green_rows, :]
 
-    source, target = iota2((64, 128), 0), iota2((64, 128), 1)
-    picked = jnp.zeros((256, 128), F32)
+    source, target = iota2((64, 384), 0), iota2((64, 384), 1)
+    picked = jnp.zeros((256, 384), F32)
     for j in range(6):
-        spots = ((target // 16 == j) & (source == x * 16 + target % 16)).astype(BF16)
+        spots = (target == source + j * 64).astype(BF16)
         picked += jnp.dot(g_wide[j].reshape(256, 64), spots, preferred_element_type=F32)
-    g_out[...] = picked.astype(BF16).reshape(16, 16, 128)
+    g_out[...] = picked.astype(BF16).reshape(16, 16, 384)
     g_in[pair] = g_out[pair]
+
+    first, second = iota2((256, 256), 0), iota2((256, 256), 1)
+    swap = ((first % 16) * 16 + first // 16 == second).astype(BF16)
+    load_three.wait()
+
+    for chunk in range(8):
+        at = pl.ds(chunk * 16, 16)
+        block = three[at].reshape(256, 384)
+        by_mu[:, at] = jnp.dot(swap, block, preferred_element_type=F32).astype(BF16).reshape(16, 16, 384)
+
+    def arrange(out):
+        for two in range(8):
+            pieces = by_mu[2 * two:2 * two + 2].reshape(256, 384)
+            block = lax.dot_general(left[...], pieces, NT, preferred_element_type=F32)
+            both = [block[:, :128].reshape(16, 24, 128), block[:, 128:].reshape(16, 24, 128)]
+            out[:, two * 48:two * 48 + 48] = jnp.concatenate(both, axis=1).astype(BF16)
+
+    unit = (iota2((384, 384), 0) == iota2((384, 384), 1)).astype(BF16)
+    left[...] = unit
+    arrange(stage)
     load_rows.wait()
     pl.semaphore_wait(barrier, 30)
 
-    for q in ORDER:
+    def offer(q):
         for dx in range(4):
             if q or dx:
                 peer = ((y + 4 - q) % 4) * 4 + (x + dx) % 4
                 remote(row_piece, rows.at[z, core, mine], a_send, a_recv.at[q], (pair, peer)).start()
 
+    offer(ORDER[0])
+
     @pl.loop(1, 16)
     def _(step):
         peer = pair_peer(step)
         remote(g_out.at[peer], g_in.at[pair], g_send, g_recv, (peer, ri)).start()
 
+    for q in ORDER[1:]:
+        offer(q)
+
     own_columns = pl.ds(pl.multiple_of(ri * 128, 128), 128)
     eye = (iota2((128, 128), 0) == iota2((128, 128), 1)).astype(BF16)
 
-    @pl.loop(0, 16)
-    def _(peer):
+    for peer in range(16):
         t_out[peer] = lax.dot_general(eye, stage[peer], NT, preferred_element_type=F32).astype(BF16)
 
     def part_of(step, which, q, count=64):
@@ -164,27 +165,25 @@
             ring(way, 1, q).start()
         own_side(q).start()
 
+    def send_three(step):
+        peer = plane_peer(step)
+        remote(t_out.at[peer], columns.at[own_columns], t_send, t_recv, (pair, peer)).start()
+
     begin(ORDER[0])
+    pl.loop(1, 8)(send_three)
 
     wait_bytes(g_in.at[pl.ds(0, 15)], g_recv)
     for k in range(6):
         g_own[k] = g_in[tiles_ref[k, pair]]
-    g_place = g_all.at[:, y, :, pl.ds(pl.multiple_of(x * 128, 128), 128)]
 
     def share(step):
-        return remote(g_own, g_place, c_send.at[step], c_recv.at[step], (pair, plane_peer(step)))
-
-    @pl.loop(1, 16)
-    def _(step):
+        peer = ((y + step) % 4) * 4 + x
+        return remote(g_own, g_all.at[:, y], c_send.at[step], c_recv.at[step], (pair, peer))
+
+    for step in (1, 3, 2):
         share(step).start()
-
-    g_all[:, y, :, pl.ds(pl.multiple_of(x * 128, 128), 128)] = g_own[...]
-
-    @pl.loop(1, 16)
-    def _(step):
-        peer = plane_peer(step)
-        remote(t_out.at[peer], columns.at[own_columns], t_send, t_recv, (pair, peer)).start()
-
+    g_all[:, y] = g_own[...]
+    pl.loop(8, 16)(send_three)
     columns[own_columns, :] = t_out[ri]
     for q in ORDER[1:]:
         begin(q)
@@ -211,17 +210,9 @@
 
     serve(1)
 
-    @pl.loop(1, 16)
-    def _(step):
+    for step in (1, 3, 2):
         share(step).wait_recv()
-
-    source, target = iota2((512, 384), 0), iota2((512, 384), 1)
-    order = (
-        (source // 128 == (target // 16) % 4) & ((source % 128) // 16 == target // 64) & (source % 16 == target % 16)
-    ).astype(BF16)
-    coupling = jnp.dot(g_all[...].reshape(384, 512), order, preferred_element_type=F32).astype(BF16)
-    for odd in range(2):
-        place[odd] = lax.dot_general(place[odd], coupling, NT, preferred_element_type=F32).astype(BF16)
+    left[...] = lax.dot_general(unit, g_all[...].reshape(384, 384), NT, preferred_element_type=F32).astype(BF16)
     arrange(h_out)
     own_lanes = pl.ds(pl.multiple_of(ri * 128, 128), 128)
 
@@ -253,8 +244,7 @@
     gram = jnp.dot(halves[...], weighted[...].reshape(2048, 384), preferred_element_type=F32)
 
     masked = jnp.where(iota2((384, 384), 0) % 24 == iota2((384, 384), 1) % 24, gram, 0.0)
-    fold = (iota2((16, 384), 1) // 24 == iota2((16, 384), 0)).astype(F32)
-    folded = jnp.dot(fold, masked, preferred_element_type=F32, precision=lax.Precision.HIGHEST)
+    folded = jnp.sum(masked.reshape(16, 24, 384), axis=1)
     spread = (iota2((384, 128), 0) // 24 == iota2((384, 128), 1) % 16).astype(F32)
     wide = jnp.dot(folded, spread, preferred_element_type=F32, precision=lax.Precision.HIGHEST)
     keep = iota2((16, 128), 1) // 16 == iota2((16, 128), 0) % 8
@@ -283,10 +273,8 @@
                 ring(way, step, q).wait_send()
                 side(way, step, q).wait_send()
 
-    @pl.loop(1, 16)
-    def _(step):
+    for step in (1, 3, 2):
         share(step).wait_send()
-
     wait_bytes(partials.at[pl.ds(0, 15)], f_send.at[0])
     wait_bytes(totals.at[pl.ds(0, 15)], f_send.at[1])
     wait_bytes(totals.at[pl.ds(0, 15)], f_recv.at[1])
@@ -313,7 +301,7 @@
             pltpu.VMEM((128, 16, 384), BF16),
             pltpu.VMEM((16, 64, 64), BF16),
             pltpu.VMEM((16, 128, 384), BF16),
-            pltpu.VMEM((2, 768, 384), BF16),
+            pltpu.VMEM((384, 384), BF16),
             pltpu.VMEM((16, 384, 128), BF16),
             pltpu.VMEM((16, 128, 384), BF16),
             pltpu.VMEM((16, 384, 128), BF16),
@@ -322,15 +310,15 @@
             pltpu.VMEM((16, 128, 384), BF16),
             pltpu.VMEM((384, 2048), BF16),
             pltpu.VMEM((6, 16, 16, 64), BF16),
-            pltpu.VMEM((16, 16, 128), BF16),
-            pltpu.VMEM((16, 16, 128), BF16),
-            pltpu.VMEM((6, 16, 128), BF16),
-            pltpu.VMEM((6, 4, 16, 512), BF16),
+            pltpu.VMEM((16, 16, 384), BF16),
+            pltpu.VMEM((16, 16, 384), BF16),
+            pltpu.VMEM((6, 16, 384), BF16),
+            pltpu.VMEM((6, 4, 16, 384), BF16),
             pltpu.VMEM((16, 2, 128), F32),
             pltpu.VMEM((16, 2, 128), F32),
             dma((5,)), dma, dma((4,)), dma, dma, dma, dma,
             dma((2, 4, 4)), dma((2, 4, 4)), dma((2, 4, 4)), dma((2, 4, 4)), dma((4,)), dma((4,)),
-            dma, dma, dma((16,)), dma((16,)), dma((2,)), dma((2,)),
+            dma, dma, dma((4,)), dma((4,)), dma((2,)), dma((2,)),
         ],
         compiler_params=pltpu.CompilerParams(
             collective_id=0, has_side_effects=True, vmem_limit_bytes=60 * 1024 * 1024

time: 82.2 us -> 76.1 us (0.926)
  Pallas kernels: 80.7 us -> 74.6 us
    pallas_call x1, Pallas kernels: 80.7 us -> 74.6 us  [on_device(): pl.pallas_call(kernel, out_shape=jax.ShapeDtypeStruct((1, 16, 16), F32),...]
where the time goes in v2:
time: 76.1 us; the launch traced here: 75.9 us
  Pallas kernels  74.6 us (98%)
  local copies, waits for them, and re-layouts  1.3 us (2%)
    pallas_call x1, Pallas kernels, on_device(): pl.pallas_call(kernel, out_shape=jax.ShapeDtypeStruct((1, 16, 16), F32),...  74.6 us

profile of v2, /device:TPU:1, one launch (start us, length us, event | category | flops | bytes accessed | tf_op | source)
XLA Modules:
  0.0 75.9 jit_solution(432998397882692871)
XLA Ops:
  0.0 74.6 %shard_map.55 = f32[1,16,16]{2,1,0:T(8,128)} custom-call(s32[6,16]{1,0:T(8,128)} %bitcast.1, s32[16]{0:T(128)} %owner_hbm.1, bf16[1,128,16,384]{3,2,1,0:T(8,128)(2,1)} %three_hbm.1, bf16[1,16,64,64]{3,2,1,0:T(8,128)(2,1)} %green_hbm.1, bf16[128,2048]{1,0:T(8,128)(2,1)} %screened_hbm.1), custom_call_target="tpu_custom_call" | custom-call | tf_op jit(solution)/shard_map/pallas_call | solution.py:293
  74.6 1.3 %copy.7 = f32[1,16,16]{2,1,0:T(8,128)} copy(f32[1,16,16]{2,1,0:T(8,128)} %shard_map.55) | data formatting | bytes 2048

commit v3 on v2

--- a/solution.py
+++ b/solution.py
@@ -93,6 +93,25 @@
     g_out[...] = picked.astype(BF16).reshape(16, 16, 384)
     g_in[pair] = g_out[pair]
 
+    load_rows.wait()
+    pl.semaphore_wait(barrier, 30)
+
+    def offer(q):
+        for dx in range(4):
+            if q or dx:
+                peer = ((y + 4 - q) % 4) * 4 + (x + dx) % 4
+                remote(row_piece, rows.at[z, core, mine], a_send, a_recv.at[q], (pair, peer)).start()
+
+    offer(ORDER[0])
+
+    @pl.loop(1, 16)
+    def _(step):
+        peer = pair_peer(step)
+        remote(g_out.at[peer], g_in.at[pair], g_send, g_recv, (peer, ri)).start()
+
+    for q in ORDER[1:]:
+        offer(q)
+
     first, second = iota2((256, 256), 0), iota2((256, 256), 1)
     swap = ((first % 16) * 16 + first // 16 == second).astype(BF16)
     load_three.wait()
@@ -112,25 +131,6 @@
     unit = (iota2((384, 384), 0) == iota2((384, 384), 1)).astype(BF16)
     left[...] = unit
     arrange(stage)
-    load_rows.wait()
-    pl.semaphore_wait(barrier, 30)
-
-    def offer(q):
-        for dx in range(4):
-            if q or dx:
-                peer = ((y + 4 - q) % 4) * 4 + (x + dx) % 4
-                remote(row_piece, rows.at[z, core, mine], a_send, a_recv.at[q], (pair, peer)).start()
-
-    offer(ORDER[0])
-
-    @pl.loop(1, 16)
-    def _(step):
-        peer = pair_peer(step)
-        remote(g_out.at[peer], g_in.at[pair], g_send, g_recv, (peer, ri)).start()
-
-    for q in ORDER[1:]:
-        offer(q)
-
     own_columns = pl.ds(pl.multiple_of(ri * 128, 128), 128)
     eye = (iota2((128, 128), 0) == iota2((128, 128), 1)).astype(BF16)
 

time: 76.1 us -> 75.8 us (level)
  no operation moved by 1% of the time
where the time goes in v3:
time: 75.8 us; the launch traced here: 75.6 us
  Pallas kernels  74.3 us (98%)
  local copies, waits for them, and re-layouts  1.3 us (2%)
    pallas_call x1, Pallas kernels, on_device(): pl.pallas_call(kernel, out_shape=jax.ShapeDtypeStruct((1, 16, 16), F32),...  74.3 us

profile of v3, /device:TPU:1, one launch (start us, length us, event | category | flops | bytes accessed | tf_op | source)
XLA Modules:
  0.0 75.6 jit_solution(14903925703114179232)
XLA Ops:
  0.0 74.3 %shard_map.55 = f32[1,16,16]{2,1,0:T(8,128)} custom-call(s32[6,16]{1,0:T(8,128)} %bitcast.1, s32[16]{0:T(128)} %owner_hbm.1, bf16[1,128,16,384]{3,2,1,0:T(8,128)(2,1)} %three_hbm.1, bf16[1,16,64,64]{3,2,1,0:T(8,128)(2,1)} %green_hbm.1, bf16[128,2048]{1,0:T(8,128)(2,1)} %screened_hbm.1), custom_call_target="tpu_custom_call" | custom-call | tf_op jit(solution)/shard_map/pallas_call | solution.py:293
  74.3 1.3 %copy.7 = f32[1,16,16]{2,1,0:T(8,128)} copy(f32[1,16,16]{2,1,0:T(8,128)} %shard_map.55) | data formatting | bytes 2048

commit v4 on v3

--- a/solution.py
+++ b/solution.py
@@ -30,8 +30,8 @@
 
 
 def kernel(
-    tiles_hbm, owner_hbm, three_hbm, green_hbm, screened_hbm, out_ref,
-    tiles_ref, owner_ref, three, green, by_mu, left, stage, t_out, h_out, columns, rows, weighted, halves,
+    tables_hbm, three_hbm, green_hbm, screened_hbm, out_ref,
+    tiles_ref, three, green, by_mu, left, stage, t_out, h_out, columns, rows, weighted, halves,
     g_wide, g_out, g_in, g_own, g_all, partials, totals,
     local_sem, a_send, a_recv, t_send, t_recv, h_send, h_recv,
     ring_send, ring_recv, sib_send, sib_recv, own_send, own_recv,
@@ -56,8 +56,7 @@
 
     load_three = pltpu.make_async_copy(three_hbm.at[0], three, local_sem.at[0])
     load_green = pltpu.make_async_copy(green_hbm.at[0], green, local_sem.at[1])
-    load_tiles = pltpu.make_async_copy(tiles_hbm, tiles_ref, local_sem.at[3])
-    load_owner = pltpu.make_async_copy(owner_hbm, owner_ref, local_sem.at[4])
+    load_tiles = pltpu.make_async_copy(tables_hbm, tiles_ref, local_sem.at[3])
     mine = pl.ds(pl.multiple_of(ri * 16, 16), 16)
     row_piece = screened_hbm.at[
         pl.ds(pl.multiple_of(z * 16, 16), 16), pl.ds(pl.multiple_of(core * 1024, 1024), 1024)
@@ -67,7 +66,6 @@
     load_tiles.start()
     load_green.start()
     load_rows.start()
-    load_owner.start()
     barrier = pltpu.get_barrier_semaphore()
 
     @pl.loop(1, 16)
@@ -77,7 +75,6 @@
 
     load_green.wait()
     load_tiles.wait()
-    load_owner.wait()
     green_rows = pl.ds(pl.multiple_of(y * 16, 16), 16)
 
     @pl.loop(0, 16)
@@ -280,7 +277,7 @@
     wait_bytes(totals.at[pl.ds(0, 15)], f_recv.at[1])
     result = jnp.zeros((2, 128), F32)
     for region in range(16):
-        result += jnp.where(owner_ref[region] == pair, totals[region], 0.0)
+        result += jnp.where(tiles_ref[6, region] == pair, totals[region], 0.0)
     again = jnp.broadcast_to(result[:, None, :], (2, 8, 128)).reshape(16, 128)
     narrow = (iota2((128, 16), 0) % 16 == iota2((128, 16), 1)).astype(F32)
     out_ref[0] = jnp.dot(
@@ -290,14 +287,14 @@
 
 def on_device(three_center, green, screened, block_tile, sigma_owner):
     dma = pltpu.SemaphoreType.DMA
+    tables = jnp.concatenate([block_tile.T, sigma_owner[None]], axis=0)
     return pl.pallas_call(
         kernel,
         out_shape=jax.ShapeDtypeStruct((1, 16, 16), F32),
-        in_specs=[pl.BlockSpec(memory_space=pltpu.HBM)] * 5,
+        in_specs=[pl.BlockSpec(memory_space=pltpu.HBM)] * 4,
         out_specs=pl.BlockSpec(memory_space=pltpu.VMEM),
         scratch_shapes=[
-            pltpu.SMEM((6, 16), jnp.int32),
-            pltpu.SMEM((16,), jnp.int32),
+            pltpu.SMEM((7, 16), jnp.int32),
             pltpu.VMEM((128, 16, 384), BF16),
             pltpu.VMEM((16, 64, 64), BF16),
             pltpu.VMEM((16, 128, 384), BF16),
@@ -316,14 +313,14 @@
             pltpu.VMEM((6, 4, 16, 384), BF16),
             pltpu.VMEM((16, 2, 128), F32),
             pltpu.VMEM((16, 2, 128), F32),
-            dma((5,)), dma, dma((4,)), dma, dma, dma, dma,
+            dma((4,)), dma, dma((4,)), dma, dma, dma, dma,
             dma((2, 4, 4)), dma((2, 4, 4)), dma((2, 4, 4)), dma((2, 4, 4)), dma((4,)), dma((4,)),
             dma, dma, dma((4,)), dma((4,)), dma((2,)), dma((2,)),
         ],
         compiler_params=pltpu.CompilerParams(
-            collective_id=0, has_side_effects=True, vmem_limit_bytes=60 * 1024 * 1024
+            collective_id=0, has_side_effects=True, vmem_limit_bytes=56500000
         ),
-    )(block_tile.T, sigma_owner, three_center, green, screened)
+    )(tables, three_center, green, screened)
 
 
 def solution(mesh):

time: 75.8 us -> 75.2 us (level)
  no operation moved by 1% of the time
where the time goes in v4:
time: 75.2 us; the launch traced here: 75.1 us
  Pallas kernels  73.8 us (98%)
    pallas_call x1, Pallas kernels, on_device(): pl.pallas_call(kernel, out_shape=jax.ShapeDtypeStruct((1, 16, 16), F32),...  73.8 us

profile of v4, /device:TPU:1, one launch (start us, length us, event | category | flops | bytes accessed | tf_op | source)
XLA Modules:
  0.0 75.1 jit_solution(4309071298367899276)
XLA Ops:
  0.0 0.7 pad_add_fusion.tables_hbm
  0.7 73.8 %shard_map.55 = f32[1,16,16]{2,1,0:T(8,128)S(1)} custom-call(s32[7,16]{1,0:T(8,128)S(1)} %pad_add_fusion.tables_hbm, bf16[1,128,16,384]{3,2,1,0:T(8,128)(2,1)} %three_hbm.1, bf16[1,16,64,64]{3,2,1,0:T(8,128)(2,1)} %green_hbm.1, bf16[128,2048]{1,0:T(8,128)(2,1)} %screened_hbm.1), custom_call_target="tpu_custom_call" | custom-call | tf_op jit(solution)/shard_map/pallas_call | solution.py:291
  74.5 0.6 copy.7
